TPU v7x, 32 devices: a whole 2x2x4 slice. The times are simulated.
32 devices in a mesh: prow: 16 (over z, y, x), pcol: 2 (over core).
Axes of the slice: x: 2, y: 2, z: 4, core: 2. Of those that a mesh axis runs over, the one named last changes fastest.
Arguments:
- trailing: float32 [8192, 8192], P('prow', 'pcol'), may hold values from -48 to 48, as said below
- panel: float32 [8192, 256], P('prow', 'pcol'), may hold values from -48 to 48, as said below
Outputs:
- updated: float32 [8192, 8192], P('prow', 'pcol')
- basis_out: float32 [8192, 256], P('prow')
Inputs may be any that keep to these rules, and one draw needn't show every extreme that they name: trailing is exactly symmetric, with a positive added diagonal. panel has full column rank.
All inputs are finite; a program needn't handle non-finite values.
Results may differ from a plain program's by a relative error of at most 0.000096.
Values sent between devices are 32-bit elements; how exact they have to be, the bound alone decides.
A program may use at most 64 MiB of HBM per device.

v0:
```python
import jax
import jax.numpy as jnp
from jax import lax
from jax.sharding import PartitionSpec as P


def spread(value, axis, source):
    kept = jnp.where(lax.axis_index(axis) == source, value, 0).astype(value.dtype)
    return lax.psum(kept, axis)


def matmul(left, right):
    return jnp.dot(left, right, precision=lax.Precision.HIGHEST, preferred_element_type=jnp.float32)


def shards(trailing, panel):
    fanout_count = lax.axis_size("prow") // lax.axis_size("pcol")
    column_index = lax.axis_index("pcol")
    panel_rows = lax.all_gather(panel, "pcol", axis=1, tiled=True)
    gram_total = lax.psum(matmul(panel_rows.T, panel_rows), "prow")
    factor = jnp.linalg.cholesky(gram_total)
    basis_rows = lax.linalg.triangular_solve(
        factor, panel_rows, left_side=False, lower=True, transpose_a=True
    )
    basis_cols = jnp.concatenate(
        [
            spread(basis_rows, "prow", column_index * fanout_count + offset)
            for offset in range(fanout_count)
        ],
        0,
    )
    product = lax.psum(matmul(trailing, basis_cols), "pcol")
    projected = lax.psum(matmul(basis_rows.T, product), "prow")
    correction = product - 0.5 * matmul(basis_rows, projected)
    correction_cols = jnp.concatenate(
        [
            spread(correction, "prow", column_index * fanout_count + offset)
            for offset in range(fanout_count)
        ],
        0,
    )
    updated = trailing - matmul(basis_rows, correction_cols.T) - matmul(correction, basis_cols.T)
    return (updated, basis_rows)


def solution(mesh):
    in_specs = (P("prow", "pcol"), P("prow", "pcol"))
    out_specs = (P("prow", "pcol"), P("prow", None))
    return jax.shard_map(shards, mesh=mesh, in_specs=in_specs, out_specs=out_specs, check_vma=False)
```

profile of v0, /device:TPU:0, one launch (start us, length us, event | category | flops | bytes accessed | tf_op | source)
XLA Modules:
  0.0 715.6 jit_solution(9417852241960511879)
XLA Ops:
  7.2 2.5 all_gather.3
  9.7 1.7 fusion.12
  11.5 111.7 %all-reduce.9.cloned.1.call-done = f32[256,256]{0,1:T(8,128)} async-done(((f32[256,256]{0,1:T(8,128)}), f32[256,256]{0,1:T(8,128)}) %all-reduce.9.cloned.1.call-update) | async-done | bytes 262160 | tf_op jit(solution)/shard_map/psum | solution.py:20
  123.2 1.1 copy.5
  125.3 11.7 %cholesky.50 = f32[128,128]{1,0:T(8,128)S(1)} custom-call(f32[128,128]{1,0:T(8,128)S(1)} %cholesky.118), custom_call_target="Cholesky" | custom-call | tf_op jit(solution)/shard_map/jit(cholesky)/cholesky | solution.py:21
  137.1 9.8 %custom-call.14 = f32[1,128,128]{1,2,0:T(8,128)S(1)} custom-call(f32[1,128,128]{2,1,0:T(8,128)S(1)} %get-tuple-element.58), custom_call_target="InvertDiagBlocksLowerTriangular" | custom-call | tf_op jit(solution)/shard_map/jit(cholesky)/cholesky | solution.py:21
  147.4 11.7 %cholesky.105 = f32[128,128]{1,0:T(8,128)S(1)} custom-call(f32[128,128]{1,0:T(8,128)S(1)} %convolution_subtract_fusion.1), custom_call_target="Cholesky" | custom-call | tf_op jit(solution)/shard_map/jit(cholesky)/cholesky | solution.py:21
  161.2 4.1 while.1
  162.0 1.4 bitcast_dynamic-update-slice_fusion.2
  163.9 1.4 bitcast_dynamic-update-slice_fusion.2
  165.3 19.7 %custom-call.15 = f32[2,128,128]{1,2,0:T(8,128)S(1)} custom-call(f32[2,128,128]{2,1,0:T(8,128)S(1)} %get-tuple-element.9), custom_call_target="InvertDiagBlocksLowerTriangular" | custom-call | tf_op jit(solution)/shard_map/triangular_solve | solution.py:22
  186.4 1.2 broadcast_select_fusion.8
  187.7 1.7 pad_maximum_fusion
  189.4 170.7 %all-reduce.17.cloned.1.call-done = (f32[512,256]{0,1:T(8,128)}, f32[512,256]{0,1:T(8,128)}, f32[512,256]{0,1:T(8,128)}, f32[512,256]{0,1:T(8,128)}, f32[512,256...) async-done(((f32[512,256]{0,1:T(8,128)}, f32[512,256]{0,1:T(8,128)}, f32[512,256]{0,1:T(8,128)}, f32[512,256]{0,1:T(8,128)}, ...) | async-done | bytes 4194320 | tf_op jit(solution)/shard_map/psum | solution.py:9
  360.1 1.2 constant_dynamic-update-slice_fusion.7
  361.4 1.1 constant_dynamic-update-slice_fusion.6
  362.5 1.1 constant_dynamic-update-slice_fusion.5
  363.5 1.1 constant_dynamic-update-slice_fusion.4
  364.9 2.0 copy-done
  366.9 10.0 %convolution_bitcast_fusion = f32[512,256]{0,1:T(8,128)} fusion(f32[4096,256]{0,1:T(8,128)S(1)} %constant_dynamic-update-slice_fusion, f32[512,4096]{1,0:T(8,128)} %param.2), kind=kOutput, calls=%fused_computation.3 | convolution fusion | flops 6442450944 | bytes 13107200 | tf_op jit(solution)/shard_map/dot_general | solution.py:13
  377.0 17.7 %all-reduce.11.cloned.1.call-done = f32[512,256]{0,1:T(8,128)} async-done(((f32[512,256]{0,1:T(8,128)}), f32[512,256]{0,1:T(8,128)}) %all-reduce.11.cloned.1.call-update) | async-done | bytes 524304 | tf_op jit(solution)/shard_map/psum | solution.py:32
  394.6 2.4 fusion.10
  397.3 111.7 %all-reduce.13.cloned.1.call-done = f32[256,256]{1,0:T(8,128)} async-done(((f32[256,256]{1,0:T(8,128)}), f32[256,256]{1,0:T(8,128)}) %all-reduce.13.cloned.1.call-update) | async-done | bytes 262160 | tf_op jit(solution)/shard_map/psum | solution.py:33
  509.0 4.1 broadcast_select_fusion
  513.2 1.0 copy.7
  514.2 171.7 %all-reduce.15.cloned.1.call-done = (f32[512,256]{0,1:T(8,128)}, f32[512,256]{0,1:T(8,128)}, f32[512,256]{0,1:T(8,128)}, f32[512,256]{0,1:T(8,128)}, f32[512,256...) async-done(((f32[512,256]{0,1:T(8,128)}, f32[512,256]{0,1:T(8,128)}, f32[512,256]{0,1:T(8,128)}, f32[512,256]{0,1:T(8,128)}, ...) | async-done | bytes 4194320 | tf_op jit(solution)/shard_map/psum | solution.py:9
  685.9 1.2 constant_dynamic-update-slice_fusion.15
  687.1 1.1 constant_dynamic-update-slice_fusion.14
  688.2 1.1 constant_dynamic-update-slice_fusion.13
  689.3 1.1 constant_dynamic-update-slice_fusion.12
  690.7 7.6 %fusion.9 = f32[512,4096]{1,0:T(8,128)S(1)} fusion(f32[4096,256]{0,1:T(8,128)S(1)} %constant_dynamic-update-slice_fusion.8, f32[512,128]{0,1:T(8,128)S(1)} %fusion.4, f32[512,128]{0,1:T(8,128)S(1)} %bitcast.49), kind=kOutput, calls=%fused_computation.64 | convolution fusion | flops 6442582016 | bytes 13107200 | tf_op jit(solution)/shard_map/dot_general | solution.py:13
  698.3 10.8 %subtract_subtract_fusion = f32[512,4096]{1,0:T(8,128)} fusion(f32[512,4096]{1,0:T(8,128)S(1)} %bitcast.44, f32[512,4096]{1,0:T(8,128)S(1)} %fusion.9, f32[512,256]{0,1:T(8,128)S(1)} %get-tuple-element.61, f32[4096,256]{0,1:T(8,128)S(1)} %copy-done.1), kind=kOutput, calls=%fused_computation.2 | convolution fusion | flops 6446645248 | bytes 29884416 | tf_op jit(solution)/shard_map/dot_general | solution.py:13
  (61 shorter events, 5.8 us)
Async XLA Ops:
  7.2 116.1 %all-reduce.9.cloned.1.call-start = ((), (), s32[]{:S(2)}) async-start(), calls=%async_computation | async-start | bytes 524288 | tf_op jit(solution)/shard_map/psum | solution.py:20
  11.4 348.7 %all-reduce.17.cloned.1.call-start = ((), (), s32[]{:S(2)}) async-start(), calls=%async_computation.4 | async-start | bytes 8388608 | tf_op jit(solution)/shard_map/psum | solution.py:9
  189.4 205.2 %all-reduce.11.cloned.1.call-start = ((), (), s32[]{:S(2)}) async-start(), calls=%async_computation.1 | async-start | bytes 1048576 | tf_op jit(solution)/shard_map/psum | solution.py:32
  360.1 4.5 copy-start.9
  360.1 4.6 copy-start.7
  360.1 4.6 copy-start.5
  360.1 4.7 copy-start.3
  364.9 2.0 copy-start
  376.9 132.1 %all-reduce.13.cloned.1.call-start = ((), (), s32[]{:S(2)}) async-start(), calls=%async_computation.2 | async-start | bytes 524288 | tf_op jit(solution)/shard_map/psum | solution.py:33
  397.0 288.9 %all-reduce.15.cloned.1.call-start = ((), (), s32[]{:S(2)}) async-start(), calls=%async_computation.3 | async-start | bytes 8388608 | tf_op jit(solution)/shard_map/psum | solution.py:9
  685.9 4.5 copy-start.8
  685.9 4.6 copy-start.6
  685.9 4.6 copy-start.4
  685.9 4.7 copy-start.2
  690.5 7.7 %slice-start = ((s8[8388608]{0:T(1024)(128)(4,1)}), s8[4194304]{0:T(1024)(128)(4,1)S(1)}, s32[]{:S(2)}) async-start(s8[8388608]{0:T(1024)(128)(4,1)} %bitcast.43), calls=%async_computation.5 | async-start | bytes 8388608
  690.6 7.6 %slice-start.1 = ((s8[8388608]{0:T(1024)(128)(4,1)}), s8[4194304]{0:T(1024)(128)(4,1)S(1)}, s32[]{:S(2)}) async-start(s8[8388608]{0:T(1024)(128)(4,1)} %bitcast.43), calls=%async_computation.6 | async-start | bytes 8388608
  690.6 7.6 %copy-start.1 = (f32[4096,256]{0,1:T(8,128)S(1)}, f32[4096,256]{0,1:T(8,128)}, u32[]{:S(2)}) copy-start(f32[4096,256]{0,1:T(8,128)} %copy-done) | copy-start | bytes 12582916
Sparse Core Ops, SparseCore 0:
  13.8 109.3 all-reduce.8
  189.5 170.5 all-reduce.16
  377.0 17.5 all-reduce.10
  401.1 107.8 all-reduce.12
  515.3 170.5 all-reduce.14
where the time goes:
time: 716 us
  waiting for transfers between devices  584 us (82%)
  other arithmetic  57.6 us (8%)
  matrix products  38.5 us (5%)
  local copies, waits for them, and re-layouts  17.3 us (2%)
  between operations  15.5 us (2%)
    psum x2, waiting for transfers between devices, spread(): return lax.psum(kept, axis)  342 us
    psum x1, waiting for transfers between devices, shards(): projected = lax.psum(matmul(basis_rows.T, product), 'prow')  112 us
    psum x1, waiting for transfers between devices, shards(): gram_total = lax.psum(matmul(panel_rows.T, panel_rows), 'prow')  112 us
    dot_general x6, matrix products, matmul(): jnp.dot(left, right, precision=lax.Precision.HIGHEST, preferred_element_t...  36.6 us
    another operation x6, other arithmetic, shards(): factor = jnp.linalg.cholesky(gram_total)  34 us
    another operation x4, other arithmetic, shards(): lax.linalg.triangular_solve(factor, panel_rows, left_side=False, lower=Tr...  21.4 us
    psum x1, waiting for transfers between devices, shards(): product = lax.psum(matmul(trailing, basis_cols), 'pcol')  17.7 us
  transfers between devices with their start and end apart: 5, of which 5 were waited for; matrix products, arithmetic and copies ran while one was open for 0% of the time, Pallas kernels for 0%

commit v1 on v0

v1 whole, which is shorter than its diff:
```python
import functools
import jax
import jax.numpy as jnp
from jax import lax
from jax.experimental import pallas as pl
from jax.experimental.pallas import tpu as pltpu
from jax.sharding import PartitionSpec as P

MESH = pl.DeviceIdType.MESH
SUB = 8
PLANE = 4


def matmul(left, right):
    return jnp.dot(left, right, precision=lax.Precision.HIGHEST, preferred_element_type=jnp.float32)


def dot_exact(left, right, dims):
    return lax.dot_general(
        left, right, (dims, ((), ())), precision=lax.Precision.HIGHEST,
        preferred_element_type=jnp.float32,
    )


def split(value):
    high = value.astype(jnp.bfloat16)
    low = (value - high.astype(jnp.float32)).astype(jnp.bfloat16)
    return high, low


def dot_split(left, right, dims):
    dot = functools.partial(
        lax.dot_general, dimension_numbers=(dims, ((), ())), preferred_element_type=jnp.float32
    )
    (left_high, left_low), (right_high, right_low) = left, right
    return dot(left_high, right_high) + (dot(left_high, right_low) + dot(left_low, right_high))


NN = ((1,), (0,))
NT = ((1,), (1,))
TN = ((0,), (0,))


def factor_rows(index, work, inverse):
    width = inverse.shape[1]
    start = pl.multiple_of(index * SUB, SUB)
    rows = work[pl.ds(start, SUB), :]
    lane = lax.broadcasted_iota(jnp.int32, (SUB, width), 1)
    sub = lax.broadcasted_iota(jnp.int32, (SUB, 128), 0)
    diagonal = [
        jnp.broadcast_to(
            jnp.sum(jnp.where(lane == start + i, rows[:, :width], 0.0), axis=1, keepdims=True),
            (SUB, 128),
        )
        for i in range(SUB)
    ]
    unit = [jnp.where(sub == i, 1.0, 0.0).astype(jnp.float32) for i in range(SUB)]
    scale = jnp.zeros((SUB, 128), jnp.float32)
    for i in range(SUB):
        pivot = jnp.broadcast_to(diagonal[i][i : i + 1, :], (SUB, 128))
        root = lax.rsqrt(pivot)
        root = root * (1.5 - 0.5 * (pivot * root) * root)
        scale = jnp.where(sub == i, root, scale)
        if i + 1 < SUB:
            ratio = jnp.where(sub > i, (diagonal[i] * root) * root, 0.0)
            for k in range(i + 1, SUB):
                diagonal[k] = diagonal[k] - ratio * diagonal[k][i : i + 1, :]
            for k in range(i + 1):
                unit[k] = unit[k] - ratio * unit[k][i : i + 1, :]
    reduced = jnp.zeros_like(rows)
    for i in range(SUB):
        weight = jnp.concatenate([scale * unit[i]] * (rows.shape[1] // 128), 1)
        reduced = reduced + weight * rows[i : i + 1, :]
    inverse[pl.ds(start, SUB), :] = reduced[:, width:]
    work[...] = work[...] - dot_exact(reduced[:, :width], reduced, TN)


def kernel(planes, trailing, panel, updated, basis_out, held, pblocks, wblocks, partial, wrecv,
           gram, grecv, proj, hrecv, work, inverse, xrows, zrows,
           load_sem, store_sem, basis_sem, pz, p1, p2, ps, precv, psib, wz, w1, w2, ws, wr, wsib,
           swap_send, swap_recv):
    row, col = lax.axis_index("prow"), lax.axis_index("pcol")
    height, half = panel.shape
    width = 2 * half
    depth = row // PLANE
    place = lax.rem(row, PLANE)
    stride1 = 2 - col
    stride2 = 1 + col
    flip1 = stride1 * (1 - 2 * lax.rem(place // stride1, 2))
    flip2 = stride2 * (1 - 2 * lax.rem(place // stride2, 2))
    other = 1 - col
    near = planes // 2

    def plane_of(k):
        return lax.rem(depth + k, planes)

    load = pltpu.make_async_copy(trailing, held, load_sem)
    load.start()
    barrier = pltpu.get_barrier_semaphore()
    peers = [(plane_of(k) * PLANE + place, col) for k in range(1, planes)]
    peers += [(row + flip1, col), (row + flip2, col), (row, other)]
    for peer in peers:
        pl.semaphore_signal(barrier, inc=1, device_id=peer, device_id_type=MESH)
    pl.semaphore_wait(barrier, len(peers))

    class Gather:
        def __init__(self, blocks, sends, recv, sib):
            self.blocks, self.recv, self.sib = blocks, recv, sib
            self.sz, self.s1, self.s2, self.ss = sends

        def copy(self, block, sem, recv, to, src=None):
            ref = self.blocks.at[col, block]
            return pltpu.make_async_remote_copy(
                src_ref=ref, dst_ref=ref, send_sem=sem, recv_sem=recv.at[block],
                device_id=to, device_id_type=MESH,
            )

        def zcopy(self, k):
            return self.copy(row, self.sz.at[k], self.recv, (plane_of(k) * PLANE + place, col))

        def copy1(self, k):
            return self.copy(plane_of(k) * PLANE + place, self.s1.at[k], self.recv,
                             (row + flip1, col))

        def copy2(self, k, hop):
            return self.copy(plane_of(k) * PLANE + place + hop * flip1, self.s2.at[k, hop],
                             self.recv, (row + flip2, col))

        def copys(self, block):
            return self.copy(block, self.ss.at[block], self.sib, (row, other))

        def arrived(self, block):
            self.copy(block, self.sz.at[0], self.recv, (row, other)).wait_recv()

        def sibling_arrived(self, block):
            ref = self.blocks.at[other, block]
            pltpu.make_async_remote_copy(
                src_ref=ref, dst_ref=ref, send_sem=self.sz.at[0], recv_sem=self.sib.at[block],
                device_id=(row, other), device_id_type=MESH,
            ).wait_recv()

        def first(self):
            self.copys(row).start()
            self.copy1(0).start()
            self.copy2(0, 0).start()
            for k in range(1, planes):
                self.zcopy(k).start()

        def forward0(self, k):
            self.arrived(plane_of(k) * PLANE + place)
            self.copy1(k).start()
            self.copy2(k, 0).start()

        def forward1(self, k):
            self.arrived(plane_of(k) * PLANE + place + flip1)
            self.copy2(k, 1).start()

        def forward2(self, k):
            for hop in range(2):
                self.arrived(plane_of(k) * PLANE + place + flip2 + hop * flip1)

            @pl.when(plane_of(k) // near != col)
            def _():
                for b in range(PLANE):
                    block = plane_of(k) * PLANE + b
                    if k:
                        self.copys(block).start()
                    else:
                        @pl.when(block != row)
                        def _():
                            self.copys(block).start()

        def sibling(self, k):
            for b in range(PLANE):
                block = plane_of(k) * PLANE + b
                if k:
                    self.sibling_arrived(block)
                else:
                    @pl.when(block != row)
                    def _():
                        self.sibling_arrived(block)

        def steps(self):
            order = [0]
            for k in range(1, planes // 2 + 1):
                order += [k] if 2 * k == planes else [k, planes - k]
            out = []
            for t in range(planes + 2):
                for lag, step in ((0, self.forward0), (1, self.forward1), (2, self.forward2)):
                    if 0 <= t - lag < planes and (lag or t):
                        out.append((step, order[t - lag]))
            return out, order

        def finish(self):
            self.copys(row).wait_send()
            for k in range(planes):
                if k:
                    self.zcopy(k).wait_send()
                self.copy1(k).wait_send()
                for hop in range(2):
                    self.copy2(k, hop).wait_send()

                @pl.when(plane_of(k) // near != col)
                def _():
                    for b in range(PLANE):
                        block = plane_of(k) * PLANE + b
                        if k:
                            self.copys(block).wait_send()
                        else:
                            @pl.when(block != row)
                            def _():
                                self.copys(block).wait_send()

    def full(blocks, block):
        return jnp.concatenate([blocks[0, block], blocks[1, block]], 1)

    def swap(source, target, slot):
        return pltpu.make_async_remote_copy(
            src_ref=source, dst_ref=target, send_sem=swap_send.at[slot],
            recv_sem=swap_recv.at[slot], device_id=(row, other), device_id_type=MESH,
        )

    pgather = Gather(pblocks, (pz, p1, p2, ps), precv, psib)
    pblocks[col, row] = panel[...]
    pgather.first()
    partial[...] = jnp.zeros_like(partial)
    gram[...] = jnp.zeros_like(gram)
    load.wait()
    steps, order = pgather.steps()
    pgather.sibling_arrived(row)

    def multiply(k):
        @pl.when(plane_of(k) // near == col)
        def _():
            pgather.sibling(k)

            @pl.loop(0, PLANE)
            def _(b):
                block = plane_of(k) * PLANE + b
                columns = pl.ds(pl.multiple_of((block - col * near * PLANE) * height, height), height)
                values = full(pblocks, block)
                product = dot_split(split(held[:, columns]), split(values), NN)
                partial[0] += product[:, :half]
                partial[1] += product[:, half:]
                gram[...] += dot_exact(values, values, TN)

    for step, k in steps:
        step(k)
        if step == pgather.forward2:
            multiply(k)

    wswap = swap(partial.at[other], wrecv, 0)
    wswap.start()
    gswap = swap(gram, grecv, 1)
    gswap.start()
    wswap.wait()
    wblocks[col, row] = partial[col] + wrecv[...]
    wgather = Gather(wblocks, (wz, w1, w2, ws), wr, wsib)
    wgather.first()
    gswap.wait()
    work[:, :width] = gram[...] + grecv[...]
    work[:, width:] = jnp.where(
        lax.broadcasted_iota(jnp.int32, (width, width), 0)
        == lax.broadcasted_iota(jnp.int32, (width, width), 1), 1.0, 0.0)

    wsteps, _ = wgather.steps()
    count = width // SUB
    bounds = [count * (i + 1) // (len(wsteps) + 1) for i in range(len(wsteps) + 1)]
    begin = 0
    for i, end in enumerate(bounds):
        lax.fori_loop(begin, end, lambda j, _: (factor_rows(j, work, inverse), 0)[1], 0)
        begin = end
        if i < len(wsteps):
            step, k = wsteps[i]
            step(k)

    linv = inverse[...]
    basis = dot_exact(full(pblocks, row), linv, NT)
    gram_basis = dot_exact(basis, linv, NN)
    xrows[...] = gram_basis
    zrows[...] = basis
    basis_copy = pltpu.make_async_copy(zrows, basis_out, basis_sem)
    basis_copy.start()
    proj[...] = jnp.zeros_like(proj)
    wgather.sibling_arrived(row)

    def column_update(k):
        @pl.when(plane_of(k) // near == col)
        def _():
            wgather.sibling(k)

            @pl.loop(0, PLANE)
            def _(b):
                block = plane_of(k) * PLANE + b
                columns = pl.ds(pl.multiple_of((block - col * near * PLANE) * height, height), height)
                values = full(wblocks, block)
                held[:, columns] -= dot_split(split(xrows[...]), split(values), NT)
                proj[...] += dot_exact(full(pblocks, block), values, TN)

    for k in order:
        column_update(k)
    hswap = swap(proj, hrecv, 2)
    hswap.start()
    hswap.wait()
    total = proj[...] + hrecv[...]
    rest = full(wblocks, row) - dot_exact(xrows[...], total, NN)
    basis_copy.wait()
    zrows[...] = dot_exact(dot_exact(rest, linv, NT), linv, NN)
    blocks = near * PLANE
    stores = []
    for b in range(blocks):
        columns = pl.ds(b * height, height)
        values = full(pblocks, col * blocks + b)
        held[:, columns] -= dot_split(split(zrows[...]), split(values), NT)
        store = pltpu.make_async_copy(held.at[:, columns], updated.at[:, columns], store_sem.at[b])
        store.start()
        stores.append(store)
    pgather.finish()
    wgather.finish()
    for store in stores:
        store.wait()


def fused(trailing, panel, rows, interpret=False):
    height, half = panel.shape
    width = 2 * half
    planes = rows // PLANE
    blocks = (2, rows, height, half)
    dma = pltpu.SemaphoreType.DMA
    vmem = lambda *shape: pltpu.VMEM(shape, jnp.float32)
    gather_sems = [dma((planes,)), dma((planes,)), dma((planes, 2)), dma((rows,)), dma((rows,)),
                   dma((rows,))]
    return pl.pallas_call(
        functools.partial(kernel, planes),
        out_shape=(jax.ShapeDtypeStruct(trailing.shape, jnp.float32),
                   jax.ShapeDtypeStruct((height, width), jnp.float32)),
        in_specs=[pl.BlockSpec(memory_space=pl.ANY), pl.BlockSpec(memory_space=pltpu.VMEM)],
        out_specs=[pl.BlockSpec(memory_space=pl.ANY), pl.BlockSpec(memory_space=pl.ANY)],
        scratch_shapes=[
            vmem(*trailing.shape), vmem(*blocks), vmem(*blocks), vmem(2, height, half),
            vmem(height, half), vmem(width, width), vmem(width, width), vmem(width, width),
            vmem(width, width), vmem(width, 2 * width), vmem(width, width), vmem(height, width),
            vmem(height, width),
            dma, dma((rows // 2,)), dma, *gather_sems, *gather_sems, dma((3,)), dma((3,)),
        ],
        compiler_params=pltpu.CompilerParams(
            collective_id=0, has_side_effects=True, vmem_limit_bytes=56 * 2**20
        ),
        name="panel_update",
    )(trailing, panel)


def shards(trailing, panel):
    rows, cols = lax.axis_size("prow"), lax.axis_size("pcol")
    if cols == 2 and rows % (2 * PLANE) == 0 and panel.shape[1] % 128 == 0:
        return tuple(fused(trailing, panel, rows))
    gather = lambda value: lax.all_to_all(
        lax.all_gather(value, "prow", axis=0, tiled=True), "pcol", 0, 1, tiled=True
    )
    panel_rows = lax.all_gather(panel, "pcol", axis=1, tiled=True)
    panel_cols = gather(panel)
    gram = lax.psum(matmul(panel_cols.T, panel_cols), "pcol")
    factor = jnp.linalg.cholesky(gram)
    solve = functools.partial(
        lax.linalg.triangular_solve, factor, left_side=False, lower=True, transpose_a=True
    )
    basis_rows, basis_cols = solve(panel_rows), solve(panel_cols)
    part = lax.psum_scatter(
        matmul(trailing, basis_cols), "pcol", scatter_dimension=1, tiled=True
    )
    product_rows = lax.all_gather(part, "pcol", axis=1, tiled=True)
    product_cols = gather(part)
    projected = lax.psum(matmul(basis_cols.T, product_cols), "pcol")
    correction = product_rows - 0.5 * matmul(basis_rows, projected)
    correction_cols = product_cols - 0.5 * matmul(basis_cols, projected)
    updated = trailing - matmul(basis_rows, correction_cols.T) - matmul(correction, basis_cols.T)
    return (updated, basis_rows)


def solution(mesh):
    in_specs = (P("prow", "pcol"), P("prow", "pcol"))
    out_specs = (P("prow", "pcol"), P("prow", None))
    return jax.shard_map(shards, mesh=mesh, in_specs=in_specs, out_specs=out_specs, check_vma=False)
```

time: 716 us -> 149 us (0.21)
  the two profiles are of different devices: /device:TPU:0 before, /device:TPU:9 now
where the time goes in v1:
time: 149 us
  Pallas kernels  139 us (93%)
  local copies, waits for them, and re-layouts  8.63 us (6%)
    pallas_call x1, Pallas kernels, fused(): pl.pallas_call(functools.partial(kernel, planes), out_shape=(jax.ShapeDty...  139 us
    unnamed x4, local copies, waits for them, and re-layouts  8.63 us

profile of v1, /device:TPU:9, one launch (start us, length us, event | category | flops | bytes accessed | tf_op | source)
XLA Modules:
  0.0 148.7 jit_solution(18427742061603167000)
XLA Ops:
  0.6 139.4 %panel_update.1 = (f32[512,4096]{1,0:T(8,128)}, f32[512,256]{1,0:T(8,128)}) custom-call(f32[512,4096]{1,0:T(8,128)} %trailing.1, f32[512,128]{1,0:T(8,128)} %panel.1), custom_call_target="tpu_custom_call" | custom-call | tf_op jit(solution)/shard_map/panel_update/pallas_call | solution.py:333
  140.1 0.0 copy-start
  140.1 7.8 %copy.6 = f32[512,4096]{1,0:T(8,128)} copy(f32[512,4096]{1,0:T(8,128)} %get-tuple-element.4) | data formatting | bytes 16777216
  147.9 0.0 copy-done
  147.9 0.8 copy.7
Async XLA Ops:
  140.1 7.8 %copy-start = (f32[512,256]{1,0:T(8,128)S(1)}, f32[512,256]{1,0:T(8,128)}, u32[]{:S(2)}) copy-start(f32[512,256]{1,0:T(8,128)} %get-tuple-element.5) | copy-start | bytes 1572868

commit v2 on v1

--- a/solution.py
+++ b/solution.py
@@ -9,6 +9,7 @@
 MESH = pl.DeviceIdType.MESH
 SUB = 8
 PLANE = 4
+BLOCK = 128
 
 
 def matmul(left, right):
@@ -41,43 +42,58 @@
 TN = ((0,), (0,))
 
 
-def factor_rows(index, work, inverse):
-    width = inverse.shape[1]
+def factor_rows(index, lo, work, upper):
+    hi = lo + upper.shape[1] // 2 + BLOCK
     start = pl.multiple_of(index * SUB, SUB)
-    rows = work[pl.ds(start, SUB), :]
-    lane = lax.broadcasted_iota(jnp.int32, (SUB, width), 1)
-    sub = lax.broadcasted_iota(jnp.int32, (SUB, 128), 0)
+    rows = work[pl.ds(start, SUB), lo:hi]
+    lane = lax.broadcasted_iota(jnp.int32, (SUB, BLOCK), 1)
+    sub = lax.broadcasted_iota(jnp.int32, (SUB, BLOCK), 0)
     diagonal = [
         jnp.broadcast_to(
-            jnp.sum(jnp.where(lane == start + i, rows[:, :width], 0.0), axis=1, keepdims=True),
-            (SUB, 128),
+            jnp.sum(jnp.where(lane == start - lo + i, rows[:, :BLOCK], 0.0), axis=1, keepdims=True),
+            (SUB, BLOCK),
         )
         for i in range(SUB)
     ]
     unit = [jnp.where(sub == i, 1.0, 0.0).astype(jnp.float32) for i in range(SUB)]
-    scale = jnp.zeros((SUB, 128), jnp.float32)
+    pivots = diagonal[0]
     for i in range(SUB):
-        pivot = jnp.broadcast_to(diagonal[i][i : i + 1, :], (SUB, 128))
-        root = lax.rsqrt(pivot)
-        root = root * (1.5 - 0.5 * (pivot * root) * root)
-        scale = jnp.where(sub == i, root, scale)
+        pivots = jnp.where(sub == i, diagonal[i], pivots)
         if i + 1 < SUB:
-            ratio = jnp.where(sub > i, (diagonal[i] * root) * root, 0.0)
+            pivot = jnp.broadcast_to(diagonal[i][i : i + 1, :], (SUB, BLOCK))
+            ratio = jnp.where(sub > i, diagonal[i], 0.0) * pl.reciprocal(pivot)
             for k in range(i + 1, SUB):
                 diagonal[k] = diagonal[k] - ratio * diagonal[k][i : i + 1, :]
             for k in range(i + 1):
                 unit[k] = unit[k] - ratio * unit[k][i : i + 1, :]
+    scale = lax.rsqrt(pivots)
+    scale = scale * (1.5 - 0.5 * (pivots * scale) * scale)
     reduced = jnp.zeros_like(rows)
     for i in range(SUB):
-        weight = jnp.concatenate([scale * unit[i]] * (rows.shape[1] // 128), 1)
+        weight = jnp.concatenate([scale * unit[i]] * (rows.shape[1] // BLOCK), 1)
         reduced = reduced + weight * rows[i : i + 1, :]
-    inverse[pl.ds(start, SUB), :] = reduced[:, width:]
-    work[...] = work[...] - dot_exact(reduced[:, :width], reduced, TN)
-
-
-def kernel(planes, trailing, panel, updated, basis_out, held, pblocks, wblocks, partial, wrecv,
-           gram, grecv, proj, hrecv, work, inverse, xrows, zrows,
-           load_sem, store_sem, basis_sem, pz, p1, p2, ps, precv, psib, wz, w1, w2, ws, wr, wsib,
+    upper[pl.ds(start, SUB), lo:hi] = reduced
+    high = reduced.astype(jnp.bfloat16).astype(jnp.float32)
+    rest = reduced - high
+    mid = rest.astype(jnp.bfloat16).astype(jnp.float32)
+    low = rest - mid
+    left = jnp.concatenate([part[:, :BLOCK] for part in (high, high, mid, high, low, mid)], 0)
+    right = jnp.concatenate([high, mid, high, low, high, mid], 0)
+    work[lo : lo + BLOCK, lo:hi] -= lax.dot_general(
+        left.astype(jnp.bfloat16), right.astype(jnp.bfloat16), (TN, ((), ())),
+        preferred_element_type=jnp.float32,
+    )
+
+
+def factor_below(lo, work, upper):
+    width = upper.shape[1] // 2
+    mid, hi = lo + BLOCK, lo + width + BLOCK
+    if mid < width:
+        work[mid:, mid:hi] -= dot_exact(upper[lo:mid, mid:width], upper[lo:mid, mid:hi], TN)
+
+
+def kernel(planes, trailing, panel, pcols, wcols, rowside, basis_out, held, pblocks, wblocks,
+           partial, wrecv, gram, grecv, proj, hrecv, work, upper, load_sem, store_sem, pz, p1, p2, ps, precv, psib, wz, w1, w2, ws, wr, wsib,
            swap_send, swap_recv):
     row, col = lax.axis_index("prow"), lax.axis_index("pcol")
     height, half = panel.shape
@@ -263,28 +279,13 @@
         lax.broadcasted_iota(jnp.int32, (width, width), 0)
         == lax.broadcasted_iota(jnp.int32, (width, width), 1), 1.0, 0.0)
 
-    wsteps, _ = wgather.steps()
-    count = width // SUB
-    bounds = [count * (i + 1) // (len(wsteps) + 1) for i in range(len(wsteps) + 1)]
-    begin = 0
-    for i, end in enumerate(bounds):
-        lax.fori_loop(begin, end, lambda j, _: (factor_rows(j, work, inverse), 0)[1], 0)
-        begin = end
-        if i < len(wsteps):
-            step, k = wsteps[i]
-            step(k)
-
-    linv = inverse[...]
-    basis = dot_exact(full(pblocks, row), linv, NT)
-    gram_basis = dot_exact(basis, linv, NN)
-    xrows[...] = gram_basis
-    zrows[...] = basis
-    basis_copy = pltpu.make_async_copy(zrows, basis_out, basis_sem)
-    basis_copy.start()
+    upper[...] = jnp.zeros_like(upper)
     proj[...] = jnp.zeros_like(proj)
-    wgather.sibling_arrived(row)
-
-    def column_update(k):
+    mine = pl.ds(col * near * PLANE, near * PLANE)
+    pstore = pltpu.make_async_copy(pblocks.at[:, mine], pcols, store_sem.at[0])
+    pstore.start()
+
+    def project(k):
         @pl.when(plane_of(k) // near == col)
         def _():
             wgather.sibling(k)
@@ -292,36 +293,74 @@
             @pl.loop(0, PLANE)
             def _(b):
                 block = plane_of(k) * PLANE + b
-                columns = pl.ds(pl.multiple_of((block - col * near * PLANE) * height, height), height)
-                values = full(wblocks, block)
-                held[:, columns] -= dot_split(split(xrows[...]), split(values), NT)
-                proj[...] += dot_exact(full(pblocks, block), values, TN)
-
+                proj[...] += dot_exact(full(pblocks, block), full(wblocks, block), TN)
+
+    wsteps, _ = wgather.steps()
     for k in order:
-        column_update(k)
+        wsteps.insert(wsteps.index((wgather.forward2, k)) + 2, (project, k))
+    wsteps.insert(0, (lambda _: wgather.sibling_arrived(row), 0))
+    count = BLOCK // SUB
+    pieces = 6
+    for lo in range(0, width, BLOCK):
+        for piece in range(pieces):
+            first, last = count * piece // pieces, count * (piece + 1) // pieces
+            lax.fori_loop(lo // SUB + first, lo // SUB + last,
+                          lambda j, _: (factor_rows(j, lo, work, upper), 0)[1], 0)
+            if wsteps:
+                step, k = wsteps.pop(0)
+                step(k)
+        factor_below(lo, work, upper)
+
+    linv = upper[:, width:]
+    basis = dot_exact(full(pblocks, row), linv, NT)
+    basis_out[...] = basis
+    rowside[:, :width] = dot_exact(basis, linv, NN)
+    for step, k in wsteps:
+        step(k)
     hswap = swap(proj, hrecv, 2)
     hswap.start()
+    wstore = pltpu.make_async_copy(wblocks.at[:, mine], wcols, store_sem.at[1])
+    wstore.start()
     hswap.wait()
     total = proj[...] + hrecv[...]
-    rest = full(wblocks, row) - dot_exact(xrows[...], total, NN)
-    basis_copy.wait()
-    zrows[...] = dot_exact(dot_exact(rest, linv, NT), linv, NN)
-    blocks = near * PLANE
-    stores = []
-    for b in range(blocks):
-        columns = pl.ds(b * height, height)
-        values = full(pblocks, col * blocks + b)
-        held[:, columns] -= dot_split(split(zrows[...]), split(values), NT)
-        store = pltpu.make_async_copy(held.at[:, columns], updated.at[:, columns], store_sem.at[b])
-        store.start()
-        stores.append(store)
+    rest = full(wblocks, row) - dot_exact(rowside[:, :width], total, NN)
+    rowside[:, width:] = dot_exact(dot_exact(rest, linv, NT), linv, NN)
     pgather.finish()
     wgather.finish()
-    for store in stores:
-        store.wait()
-
-
-def fused(trailing, panel, rows, interpret=False):
+    pstore.wait()
+    wstore.wait()
+
+
+def update_kernel(trailing, pcols, wcols, rowside, basis, updated, basis_out, high, low):
+    @pl.when(pl.program_id(0) == 0)
+    def _():
+        high[...], low[...] = split(rowside[...])
+        basis_out[...] = basis[...]
+
+    values = jnp.concatenate([wcols[0, 0], wcols[1, 0], pcols[0, 0], pcols[1, 0]], 1)
+    updated[...] = trailing[...] - dot_split((high[...], low[...]), split(values), NT)
+
+
+def update(trailing, pcols, wcols, rowside, basis):
+    height, width = basis.shape
+    _, blocks, _, half = pcols.shape
+    square = pl.BlockSpec((height, height), lambda j: (0, j))
+    column = pl.BlockSpec((2, 1, height, half), lambda j: (0, j, 0, 0))
+    whole = lambda *shape: pl.BlockSpec(shape, lambda j: (0, 0))
+    return pl.pallas_call(
+        update_kernel,
+        grid=(blocks,),
+        out_shape=(jax.ShapeDtypeStruct(trailing.shape, jnp.float32),
+                   jax.ShapeDtypeStruct(basis.shape, jnp.float32)),
+        in_specs=[square, column, column, whole(height, 2 * width), whole(height, width)],
+        out_specs=[square, whole(height, width)],
+        scratch_shapes=[pltpu.VMEM((height, 2 * width), jnp.bfloat16)] * 2,
+        compiler_params=pltpu.CompilerParams(vmem_limit_bytes=40 * 2**20),
+        name="update",
+    )(trailing, pcols, wcols, rowside, basis)
+
+
+def fused(trailing, panel, rows):
     height, half = panel.shape
     width = 2 * half
     planes = rows // PLANE
@@ -332,16 +371,17 @@
                    dma((rows,))]
     return pl.pallas_call(
         functools.partial(kernel, planes),
-        out_shape=(jax.ShapeDtypeStruct(trailing.shape, jnp.float32),
-                   jax.ShapeDtypeStruct((height, width), jnp.float32)),
+        out_shape=tuple(jax.ShapeDtypeStruct(shape, jnp.float32) for shape in (
+            (2, rows // 2, height, half), (2, rows // 2, height, half), (height, 2 * width),
+            (height, width))),
         in_specs=[pl.BlockSpec(memory_space=pl.ANY), pl.BlockSpec(memory_space=pltpu.VMEM)],
-        out_specs=[pl.BlockSpec(memory_space=pl.ANY), pl.BlockSpec(memory_space=pl.ANY)],
+        out_specs=[pl.BlockSpec(memory_space=pl.ANY)] * 2
+        + [pl.BlockSpec(memory_space=pltpu.VMEM)] * 2,
         scratch_shapes=[
             vmem(*trailing.shape), vmem(*blocks), vmem(*blocks), vmem(2, height, half),
             vmem(height, half), vmem(width, width), vmem(width, width), vmem(width, width),
-            vmem(width, width), vmem(width, 2 * width), vmem(width, width), vmem(height, width),
-            vmem(height, width),
-            dma, dma((rows // 2,)), dma, *gather_sems, *gather_sems, dma((3,)), dma((3,)),
+            vmem(width, width), vmem(width, 2 * width), vmem(width, 2 * width),
+            dma, dma((2,)), *gather_sems, *gather_sems, dma((3,)), dma((3,)),
         ],
         compiler_params=pltpu.CompilerParams(
             collective_id=0, has_side_effects=True, vmem_limit_bytes=56 * 2**20
@@ -353,7 +393,7 @@
 def shards(trailing, panel):
     rows, cols = lax.axis_size("prow"), lax.axis_size("pcol")
     if cols == 2 and rows % (2 * PLANE) == 0 and panel.shape[1] % 128 == 0:
-        return tuple(fused(trailing, panel, rows))
+        return tuple(update(trailing, *fused(trailing, panel, rows)))
     gather = lambda value: lax.all_to_all(
         lax.all_gather(value, "prow", axis=0, tiled=True), "pcol", 0, 1, tiled=True
     )

time: 149 us -> 148 us (level)
  the two profiles are of different devices: /device:TPU:9 before, /device:TPU:0 now
where the time goes in v2:
time: 148 us; the launch traced here: 145 us
  Pallas kernels  138 us (93%)
  local copies, waits for them, and re-layouts  6.63 us (4%)
    pallas_call x1, Pallas kernels, fused(): pl.pallas_call(functools.partial(kernel, planes), out_shape=tuple((jax.Sh...  125 us
    pallas_call x1, Pallas kernels, update(): pl.pallas_call(update_kernel, grid=(blocks,), out_shape=(jax.ShapeDtypeSt...  12.6 us
    unnamed x8, local copies, waits for them, and re-layouts  6.63 us

profile of v2, /device:TPU:0, one launch (start us, length us, event | category | flops | bytes accessed | tf_op | source)
XLA Modules:
  0.0 144.8 jit_solution(5064840643436021357)
XLA Ops:
  0.6 124.9 %panel_update.1 = (f32[2,8,512,128]{3,2,1,0:T(8,128)}, f32[2,8,512,128]{3,2,1,0:T(8,128)}, f32[512,512]{1,0:T(8,128)}, f32[512,256]{1,0:T(8,128)}) custom-call(f32[512,4096]{1,0:T(8,128)} %trailing.3, f32[512,128]{1,0:T(8,128)} %panel.1), custom_call_target="tpu_custom_call" | custom-call | tf_op jit(solution)/shard_map/panel_update/pallas_call | solution.py:372
  125.5 0.0 copy-start
  125.6 2.2 %copy-done = f32[2,8,512,128]{3,2,1,0:T(8,128)S(1)} copy-done((f32[2,8,512,128]{3,2,1,0:T(8,128)S(1)}, f32[2,8,512,128]{3,2,1,0:T(8,128)}, u32[]{:S(2)}) %copy-start) | copy-done | bytes 4194328
  127.7 0.0 copy-start.1
  127.7 2.2 %copy-done.1 = f32[2,8,512,128]{3,2,1,0:T(8,128)S(1)} copy-done((f32[2,8,512,128]{3,2,1,0:T(8,128)S(1)}, f32[2,8,512,128]{3,2,1,0:T(8,128)}, u32[]{:S(2)}) %copy-start.1) | copy-done | bytes 4194328
  129.9 0.0 copy-start.2
  129.9 1.2 copy-done.2
  131.2 0.0 copy-start.3
  131.2 1.0 copy-done.3
  132.2 12.6 %update.1 = (f32[512,4096]{1,0:T(8,128)}, f32[512,256]{1,0:T(8,128)}) custom-call(f32[512,4096]{1,0:T(8,128)} %trailing.3, f32[2,8,512,128]{3,2,1,0:T(8,128)S(1)} %copy-done, f32[2,8,512,128]{3,2,1,0:T(8,128)S(1)} %copy-done.1, f32[512,512]{1,0:T(8,128)S(1)} %copy-done.2, f32[512,256]{1,0:T(8,128)S(1)} %copy-done.3), custom_call_target="tpu_custom_call" | custom-call | tf_op jit(solution)/shard_map/update/pallas_call | solution.py:350
Async XLA Ops:
  125.5 2.2 %copy-start = (f32[2,8,512,128]{3,2,1,0:T(8,128)S(1)}, f32[2,8,512,128]{3,2,1,0:T(8,128)}, u32[]{:S(2)}) copy-start(f32[2,8,512,128]{3,2,1,0:T(8,128)} %get-tuple-element.6.pcols) | copy-start | bytes 12582916
  127.7 2.2 %copy-start.1 = (f32[2,8,512,128]{3,2,1,0:T(8,128)S(1)}, f32[2,8,512,128]{3,2,1,0:T(8,128)}, u32[]{:S(2)}) copy-start(f32[2,8,512,128]{3,2,1,0:T(8,128)} %get-tuple-element.7.wcols) | copy-start | bytes 12582916
  129.9 1.2 copy-start.2
  131.2 1.0 copy-start.3

commit v3 on v2

--- a/solution.py
+++ b/solution.py
@@ -10,6 +10,7 @@
 SUB = 8
 PLANE = 4
 BLOCK = 128
+CHUNKS = 2
 
 
 def matmul(left, right):
@@ -106,9 +107,14 @@
     flip2 = stride2 * (1 - 2 * lax.rem(place // stride2, 2))
     other = 1 - col
     near = planes // 2
+    chunk = height // CHUNKS
+
+    upper_half = depth // near
+    mirrored = depth + upper_half * (planes - 1 - 2 * depth)
 
     def plane_of(k):
-        return lax.rem(depth + k, planes)
+        plane = k + (1 - 2 * k) * mirrored if k < 2 else k
+        return plane + upper_half * (planes - 1 - 2 * plane)
 
     load = pltpu.make_async_copy(trailing, held, load_sem)
     load.start()
@@ -124,108 +130,103 @@
             self.blocks, self.recv, self.sib = blocks, recv, sib
             self.sz, self.s1, self.s2, self.ss = sends
 
-        def copy(self, block, sem, recv, to, src=None):
-            ref = self.blocks.at[col, block]
+        def part(self, which, block, h):
+            return self.blocks.at[which, block, pl.ds(h * chunk, chunk)]
+
+        def copy(self, which, block, h, sem, recv, to):
+            ref = self.part(which, block, h)
             return pltpu.make_async_remote_copy(
-                src_ref=ref, dst_ref=ref, send_sem=sem, recv_sem=recv.at[block],
+                src_ref=ref, dst_ref=ref, send_sem=sem, recv_sem=recv.at[block, h],
                 device_id=to, device_id_type=MESH,
             )
 
-        def zcopy(self, k):
-            return self.copy(row, self.sz.at[k], self.recv, (plane_of(k) * PLANE + place, col))
-
-        def copy1(self, k):
-            return self.copy(plane_of(k) * PLANE + place, self.s1.at[k], self.recv,
+        def zcopy(self, k, h):
+            return self.copy(col, row, h, self.sz.at[k, h], self.recv,
+                             (plane_of(k) * PLANE + place, col))
+
+        def copy1(self, k, h):
+            return self.copy(col, plane_of(k) * PLANE + place, h, self.s1.at[k, h], self.recv,
                              (row + flip1, col))
 
-        def copy2(self, k, hop):
-            return self.copy(plane_of(k) * PLANE + place + hop * flip1, self.s2.at[k, hop],
-                             self.recv, (row + flip2, col))
-
-        def copys(self, block):
-            return self.copy(block, self.ss.at[block], self.sib, (row, other))
-
-        def arrived(self, block):
-            self.copy(block, self.sz.at[0], self.recv, (row, other)).wait_recv()
-
-        def sibling_arrived(self, block):
-            ref = self.blocks.at[other, block]
-            pltpu.make_async_remote_copy(
-                src_ref=ref, dst_ref=ref, send_sem=self.sz.at[0], recv_sem=self.sib.at[block],
-                device_id=(row, other), device_id_type=MESH,
-            ).wait_recv()
+        def copy2(self, k, h, hop):
+            return self.copy(col, plane_of(k) * PLANE + place + hop * flip1, h,
+                             self.s2.at[k, hop, h], self.recv, (row + flip2, col))
+
+        def copys(self, block, h):
+            return self.copy(col, block, h, self.ss.at[block, h], self.sib, (row, other))
+
+        def arrived(self, block, h):
+            self.copy(col, block, h, self.sz.at[0, 0], self.recv, (row, other)).wait_recv()
+
+        def sibling_arrived(self, block, h):
+            self.copy(other, block, h, self.sz.at[0, 0], self.sib, (row, other)).wait_recv()
+
+        def own_arrived(self):
+            for h in range(CHUNKS):
+                self.sibling_arrived(row, h)
 
         def first(self):
-            self.copys(row).start()
-            self.copy1(0).start()
-            self.copy2(0, 0).start()
-            for k in range(1, planes):
-                self.zcopy(k).start()
-
-        def forward0(self, k):
-            self.arrived(plane_of(k) * PLANE + place)
-            self.copy1(k).start()
-            self.copy2(k, 0).start()
-
-        def forward1(self, k):
-            self.arrived(plane_of(k) * PLANE + place + flip1)
-            self.copy2(k, 1).start()
-
-        def forward2(self, k):
-            for hop in range(2):
-                self.arrived(plane_of(k) * PLANE + place + flip2 + hop * flip1)
-
-            @pl.when(plane_of(k) // near != col)
-            def _():
-                for b in range(PLANE):
-                    block = plane_of(k) * PLANE + b
-                    if k:
-                        self.copys(block).start()
-                    else:
-                        @pl.when(block != row)
-                        def _():
-                            self.copys(block).start()
-
-        def sibling(self, k):
+            for h in range(CHUNKS):
+                self.copy1(0, h).start()
+                self.copy2(0, h, 0).start()
+                for k in range(1, planes):
+                    self.zcopy(k, h).start()
+            for h in range(CHUNKS):
+                self.copys(row, h).start()
+
+        def forward0(self, k, h):
+            self.arrived(plane_of(k) * PLANE + place, h)
+            self.copy1(k, h).start()
+            self.copy2(k, h, 0).start()
+
+        def forward1(self, k, h):
+            self.arrived(plane_of(k) * PLANE + place + flip1, h)
+            self.copy2(k, h, 1).start()
+
+        def others(self, k, act):
             for b in range(PLANE):
                 block = plane_of(k) * PLANE + b
                 if k:
-                    self.sibling_arrived(block)
+                    act(block)
                 else:
-                    @pl.when(block != row)
+                    pl.when(block != row)(functools.partial(act, block))
+
+        def forward2(self, k, h):
+            for hop in range(2):
+                self.arrived(plane_of(k) * PLANE + place + flip2 + hop * flip1, h)
+
+            @pl.when(plane_of(k) // near != col)
+            def _():
+                self.others(k, lambda block: self.copys(block, h).start())
+
+        def sibling(self, k):
+            for h in range(CHUNKS):
+                self.others(k, lambda block: self.sibling_arrived(block, h))
+
+        def steps(self):
+            items = [(k, h) for k in range(planes) for h in range(CHUNKS)]
+            out = []
+            for t in range(len(items) + 2):
+                for lag, step in ((0, self.forward0), (1, self.forward1), (2, self.forward2)):
+                    if 0 <= t - lag < len(items):
+                        k, h = items[t - lag]
+                        if lag or k:
+                            out.append((step, (k, h)))
+            return out
+
+        def finish(self):
+            for h in range(CHUNKS):
+                self.copys(row, h).wait_send()
+                for k in range(planes):
+                    if k:
+                        self.zcopy(k, h).wait_send()
+                    self.copy1(k, h).wait_send()
+                    for hop in range(2):
+                        self.copy2(k, h, hop).wait_send()
+
+                    @pl.when(plane_of(k) // near != col)
                     def _():
-                        self.sibling_arrived(block)
-
-        def steps(self):
-            order = [0]
-            for k in range(1, planes // 2 + 1):
-                order += [k] if 2 * k == planes else [k, planes - k]
-            out = []
-            for t in range(planes + 2):
-                for lag, step in ((0, self.forward0), (1, self.forward1), (2, self.forward2)):
-                    if 0 <= t - lag < planes and (lag or t):
-                        out.append((step, order[t - lag]))
-            return out, order
-
-        def finish(self):
-            self.copys(row).wait_send()
-            for k in range(planes):
-                if k:
-                    self.zcopy(k).wait_send()
-                self.copy1(k).wait_send()
-                for hop in range(2):
-                    self.copy2(k, hop).wait_send()
-
-                @pl.when(plane_of(k) // near != col)
-                def _():
-                    for b in range(PLANE):
-                        block = plane_of(k) * PLANE + b
-                        if k:
-                            self.copys(block).wait_send()
-                        else:
-                            @pl.when(block != row)
-                            def _():
-                                self.copys(block).wait_send()
+                        self.others(k, lambda block: self.copys(block, h).wait_send())
 
     def full(blocks, block):
         return jnp.concatenate([blocks[0, block], blocks[1, block]], 1)
@@ -242,8 +243,7 @@
     partial[...] = jnp.zeros_like(partial)
     gram[...] = jnp.zeros_like(gram)
     load.wait()
-    steps, order = pgather.steps()
-    pgather.sibling_arrived(row)
+    pgather.own_arrived()
 
     def multiply(k):
         @pl.when(plane_of(k) // near == col)
@@ -260,9 +260,9 @@
                 partial[1] += product[:, half:]
                 gram[...] += dot_exact(values, values, TN)
 
-    for step, k in steps:
-        step(k)
-        if step == pgather.forward2:
+    for step, (k, h) in pgather.steps():
+        step(k, h)
+        if step == pgather.forward2 and h == CHUNKS - 1:
             multiply(k)
 
     wswap = swap(partial.at[other], wrecv, 0)
@@ -295,28 +295,29 @@
                 block = plane_of(k) * PLANE + b
                 proj[...] += dot_exact(full(pblocks, block), full(wblocks, block), TN)
 
-    wsteps, _ = wgather.steps()
-    for k in order:
-        wsteps.insert(wsteps.index((wgather.forward2, k)) + 2, (project, k))
-    wsteps.insert(0, (lambda _: wgather.sibling_arrived(row), 0))
+    wsteps = wgather.steps()
+    for k in range(planes):
+        wsteps.insert(wsteps.index((wgather.forward2, (k, CHUNKS - 1))) + 2, (project, (k,)))
+    wsteps.insert(0, (wgather.own_arrived, ()))
     count = BLOCK // SUB
-    pieces = 6
+    pieces = 8
+    each = -(-len(wsteps) // (pieces * (width // BLOCK)))
     for lo in range(0, width, BLOCK):
         for piece in range(pieces):
             first, last = count * piece // pieces, count * (piece + 1) // pieces
             lax.fori_loop(lo // SUB + first, lo // SUB + last,
                           lambda j, _: (factor_rows(j, lo, work, upper), 0)[1], 0)
-            if wsteps:
-                step, k = wsteps.pop(0)
-                step(k)
+            for step, at in wsteps[:each]:
+                step(*at)
+            wsteps = wsteps[each:]
         factor_below(lo, work, upper)
 
     linv = upper[:, width:]
     basis = dot_exact(full(pblocks, row), linv, NT)
     basis_out[...] = basis
     rowside[:, :width] = dot_exact(basis, linv, NN)
-    for step, k in wsteps:
-        step(k)
+    for step, at in wsteps:
+        step(*at)
     hswap = swap(proj, hrecv, 2)
     hswap.start()
     wstore = pltpu.make_async_copy(wblocks.at[:, mine], wcols, store_sem.at[1])
@@ -331,14 +332,25 @@
     wstore.wait()
 
 
-def update_kernel(trailing, pcols, wcols, rowside, basis, updated, basis_out, high, low):
+def update_kernel(trailing, pcols, wcols, rowside, basis, updated, basis_out, left, right):
+    depth = rowside.shape[1]
+
     @pl.when(pl.program_id(0) == 0)
     def _():
-        high[...], low[...] = split(rowside[...])
+        high, low = split(rowside[...])
+        left[:, :depth], left[:, depth : 2 * depth], left[:, 2 * depth :] = high, high, low
         basis_out[...] = basis[...]
 
-    values = jnp.concatenate([wcols[0, 0], wcols[1, 0], pcols[0, 0], pcols[1, 0]], 1)
-    updated[...] = trailing[...] - dot_split((high[...], low[...]), split(values), NT)
+    for i, ref in enumerate((wcols, pcols)):
+        for j in range(2):
+            half = ref.shape[3]
+            high, low = split(ref[j, 0])
+            for part, value in enumerate((high, low, high)):
+                start = part * depth + (2 * i + j) * half
+                right[:, start : start + half] = value
+    updated[...] = trailing[...] - lax.dot_general(
+        left[...], right[...], (NT, ((), ())), preferred_element_type=jnp.float32
+    )
 
 
 def update(trailing, pcols, wcols, rowside, basis):
@@ -354,8 +366,8 @@
                    jax.ShapeDtypeStruct(basis.shape, jnp.float32)),
         in_specs=[square, column, column, whole(height, 2 * width), whole(height, width)],
         out_specs=[square, whole(height, width)],
-        scratch_shapes=[pltpu.VMEM((height, 2 * width), jnp.bfloat16)] * 2,
-        compiler_params=pltpu.CompilerParams(vmem_limit_bytes=40 * 2**20),
+        scratch_shapes=[pltpu.VMEM((height, 6 * width), jnp.bfloat16)] * 2,
+        compiler_params=pltpu.CompilerParams(vmem_limit_bytes=60 * 2**20),
         name="update",
     )(trailing, pcols, wcols, rowside, basis)
 
@@ -367,8 +379,8 @@
     blocks = (2, rows, height, half)
     dma = pltpu.SemaphoreType.DMA
     vmem = lambda *shape: pltpu.VMEM(shape, jnp.float32)
-    gather_sems = [dma((planes,)), dma((planes,)), dma((planes, 2)), dma((rows,)), dma((rows,)),
-                   dma((rows,))]
+    gather_sems = [dma((planes, CHUNKS)), dma((planes, CHUNKS)), dma((planes, 2, CHUNKS)),
+                   dma((rows, CHUNKS)), dma((rows, CHUNKS)), dma((rows, CHUNKS))]
     return pl.pallas_call(
         functools.partial(kernel, planes),
         out_shape=tuple(jax.ShapeDtypeStruct(shape, jnp.float32) for shape in (
@@ -392,7 +404,7 @@
 
 def shards(trailing, panel):
     rows, cols = lax.axis_size("prow"), lax.axis_size("pcol")
-    if cols == 2 and rows % (2 * PLANE) == 0 and panel.shape[1] % 128 == 0:
+    if cols == 2 and rows == 4 * PLANE and panel.shape[1] % 128 == 0:
         return tuple(update(trailing, *fused(trailing, panel, rows)))
     gather = lambda value: lax.all_to_all(
         lax.all_gather(value, "prow", axis=0, tiled=True), "pcol", 0, 1, tiled=True

time: 148 us -> 128 us (0.86); the launches traced: 145 us -> 128 us
  Pallas kernels: 138 us -> 128 us
  local copies, waits for them, and re-layouts: 6.63 us -> 0 us
    pallas_call x1, Pallas kernels: 125 us -> 113 us  [fused(): pl.pallas_call(functools.partial(kernel, planes), out_shape=tuple((jax.Sh...]
    unnamed x8 -> x0, local copies, waits for them, and re-layouts: 6.63 us -> none
    pallas_call x1, Pallas kernels: 12.6 us -> 14.8 us  [update(): pl.pallas_call(update_kernel, grid=(blocks,), out_shape=(jax.ShapeDtypeSt...]
where the time goes in v3:
time: 128 us
  Pallas kernels  128 us (100%)
    pallas_call x1, Pallas kernels, fused(): pl.pallas_call(functools.partial(kernel, planes), out_shape=tuple((jax.Sh...  113 us
    pallas_call x1, Pallas kernels, update(): pl.pallas_call(update_kernel, grid=(blocks,), out_shape=(jax.ShapeDtypeSt...  14.8 us

profile of v3, /device:TPU:0, one launch (start us, length us, event | category | flops | bytes accessed | tf_op | source)
XLA Modules:
  0.0 128.2 jit_solution(7970237653616548577)
XLA Ops:
  0.6 112.7 %panel_update.1 = (f32[2,8,512,128]{3,2,1,0:T(8,128)}, f32[2,8,512,128]{3,2,1,0:T(8,128)}, f32[512,512]{1,0:T(8,128)}, f32[512,256]{1,0:T(8,128)}) custom-call(f32[512,4096]{1,0:T(8,128)} %trailing.3, f32[512,128]{1,0:T(8,128)} %panel.1), custom_call_target="tpu_custom_call" | custom-call | tf_op jit(solution)/shard_map/panel_update/pallas_call | solution.py:384
  113.4 14.8 %update.1 = (f32[512,4096]{1,0:T(8,128)}, f32[512,256]{1,0:T(8,128)}) custom-call(f32[512,4096]{1,0:T(8,128)} %trailing.3, f32[2,8,512,128]{3,2,1,0:T(8,128)} %get-tuple-element.6.pcols, f32[2,8,512,128]{3,2,1,0:T(8,128)} %get-tuple-element.7.wcols, f32[512,512]{1,0:T(8,128)} %get-tuple-element.8.rowside, f32[512,256]{1,0:T(8,128)} %get-tuple-element.9.basis), custom_call_target="tpu_custom_call" | custom-call | tf_op jit(solution)/shard_map/update/pallas_call | solution.py:362

commit v4 on v3

--- a/solution.py
+++ b/solution.py
@@ -174,45 +174,57 @@
             for h in range(CHUNKS):
                 self.copys(row, h).start()
 
+        def offset(self, k, i):
+            return plane_of(k) * PLANE + place + lax.rem(i, 2) * flip1 + i // 2 * flip2
+
+        def hand_over(self, k, h, i):
+            @pl.when(plane_of(k) // near != col)
+            def _():
+                self.copys(self.offset(k, i), h).start()
+
         def forward0(self, k, h):
-            self.arrived(plane_of(k) * PLANE + place, h)
+            self.arrived(self.offset(k, 0), h)
             self.copy1(k, h).start()
             self.copy2(k, h, 0).start()
+            self.hand_over(k, h, 0)
 
         def forward1(self, k, h):
-            self.arrived(plane_of(k) * PLANE + place + flip1, h)
+            self.arrived(self.offset(k, 1), h)
             self.copy2(k, h, 1).start()
-
-        def others(self, k, act):
-            for b in range(PLANE):
-                block = plane_of(k) * PLANE + b
-                if k:
-                    act(block)
-                else:
-                    pl.when(block != row)(functools.partial(act, block))
+            self.hand_over(k, h, 1)
 
         def forward2(self, k, h):
-            for hop in range(2):
-                self.arrived(plane_of(k) * PLANE + place + flip2 + hop * flip1, h)
-
-            @pl.when(plane_of(k) // near != col)
-            def _():
-                self.others(k, lambda block: self.copys(block, h).start())
-
-        def sibling(self, k):
-            for h in range(CHUNKS):
-                self.others(k, lambda block: self.sibling_arrived(block, h))
-
-        def steps(self):
+            for i in (2, 3):
+                self.arrived(self.offset(k, i), h)
+                self.hand_over(k, h, i)
+
+        def steps(self, use):
+            def pair(k, g):
+                @pl.when(plane_of(k) // near == col)
+                def _():
+                    for i in (2 * g, 2 * g + 1):
+                        for h in range(CHUNKS):
+                            if k or i:
+                                self.sibling_arrived(self.offset(k, i), h)
+
+                    @pl.loop(2 * g, 2 * g + 2)
+                    def _(i):
+                        use(self.offset(k, i))
+
             items = [(k, h) for k in range(planes) for h in range(CHUNKS)]
-            out = []
+            out, ready, waiting = [(self.own_arrived, ())], [], []
             for t in range(len(items) + 2):
+                ready, waiting = ready + waiting, []
                 for lag, step in ((0, self.forward0), (1, self.forward1), (2, self.forward2)):
                     if 0 <= t - lag < len(items):
                         k, h = items[t - lag]
                         if lag or k:
                             out.append((step, (k, h)))
-            return out
+                        if lag and h == CHUNKS - 1:
+                            waiting.append((pair, (k, lag - 1)))
+                out += ready[:1]
+                ready = ready[1:]
+            return out + ready + waiting
 
         def finish(self):
             for h in range(CHUNKS):
@@ -226,7 +238,9 @@
 
                     @pl.when(plane_of(k) // near != col)
                     def _():
-                        self.others(k, lambda block: self.copys(block, h).wait_send())
+                        for i in range(PLANE):
+                            if k or i:
+                                self.copys(self.offset(k, i), h).wait_send()
 
     def full(blocks, block):
         return jnp.concatenate([blocks[0, block], blocks[1, block]], 1)
@@ -243,27 +257,17 @@
     partial[...] = jnp.zeros_like(partial)
     gram[...] = jnp.zeros_like(gram)
     load.wait()
-    pgather.own_arrived()
-
-    def multiply(k):
-        @pl.when(plane_of(k) // near == col)
-        def _():
-            pgather.sibling(k)
-
-            @pl.loop(0, PLANE)
-            def _(b):
-                block = plane_of(k) * PLANE + b
-                columns = pl.ds(pl.multiple_of((block - col * near * PLANE) * height, height), height)
-                values = full(pblocks, block)
-                product = dot_split(split(held[:, columns]), split(values), NN)
-                partial[0] += product[:, :half]
-                partial[1] += product[:, half:]
-                gram[...] += dot_exact(values, values, TN)
-
-    for step, (k, h) in pgather.steps():
-        step(k, h)
-        if step == pgather.forward2 and h == CHUNKS - 1:
-            multiply(k)
+
+    def multiply(block):
+        columns = pl.ds(pl.multiple_of((block - col * near * PLANE) * height, height), height)
+        values = full(pblocks, block)
+        product = dot_split(split(held[:, columns]), split(values), NN)
+        partial[0] += product[:, :half]
+        partial[1] += product[:, half:]
+        gram[...] += dot_exact(values, values, TN)
+
+    for step, at in pgather.steps(multiply):
+        step(*at)
 
     wswap = swap(partial.at[other], wrecv, 0)
     wswap.start()
@@ -285,20 +289,10 @@
     pstore = pltpu.make_async_copy(pblocks.at[:, mine], pcols, store_sem.at[0])
     pstore.start()
 
-    def project(k):
-        @pl.when(plane_of(k) // near == col)
-        def _():
-            wgather.sibling(k)
-
-            @pl.loop(0, PLANE)
-            def _(b):
-                block = plane_of(k) * PLANE + b
-                proj[...] += dot_exact(full(pblocks, block), full(wblocks, block), TN)
-
-    wsteps = wgather.steps()
-    for k in range(planes):
-        wsteps.insert(wsteps.index((wgather.forward2, (k, CHUNKS - 1))) + 2, (project, (k,)))
-    wsteps.insert(0, (wgather.own_arrived, ()))
+    def project(block):
+        proj[...] += dot_exact(full(pblocks, block), full(wblocks, block), TN)
+
+    wsteps = wgather.steps(project)
     count = BLOCK // SUB
     pieces = 8
     each = -(-len(wsteps) // (pieces * (width // BLOCK)))

time: 128 us -> 121 us (0.945)
  Pallas kernels: 128 us -> 120 us
    pallas_call x1, Pallas kernels: 113 us -> 106 us  [fused(): pl.pallas_call(functools.partial(kernel, planes), out_shape=tuple((jax.Sh...]
where the time goes in v4:
time: 121 us
  Pallas kernels  120 us (99%)
    pallas_call x1, Pallas kernels, fused(): pl.pallas_call(functools.partial(kernel, planes), out_shape=tuple((jax.Sh...  106 us
    pallas_call x1, Pallas kernels, update(): pl.pallas_call(update_kernel, grid=(blocks,), out_shape=(jax.ShapeDtypeSt...  14.8 us

profile of v4, /device:TPU:0, one launch (start us, length us, event | category | flops | bytes accessed | tf_op | source)
XLA Modules:
  0.0 121.0 jit_solution(12869047469025391949)
XLA Ops:
  0.6 105.6 %panel_update.1 = (f32[2,8,512,128]{3,2,1,0:T(8,128)}, f32[2,8,512,128]{3,2,1,0:T(8,128)}, f32[512,512]{1,0:T(8,128)}, f32[512,256]{1,0:T(8,128)}) custom-call(f32[512,4096]{1,0:T(8,128)} %trailing.3, f32[512,128]{1,0:T(8,128)} %panel.1), custom_call_target="tpu_custom_call" | custom-call | tf_op jit(solution)/shard_map/panel_update/pallas_call | solution.py:378
  106.2 14.8 %update.1 = (f32[512,4096]{1,0:T(8,128)}, f32[512,256]{1,0:T(8,128)}) custom-call(f32[512,4096]{1,0:T(8,128)} %trailing.3, f32[2,8,512,128]{3,2,1,0:T(8,128)} %get-tuple-element.6.pcols, f32[2,8,512,128]{3,2,1,0:T(8,128)} %get-tuple-element.7.wcols, f32[512,512]{1,0:T(8,128)} %get-tuple-element.8.rowside, f32[512,256]{1,0:T(8,128)} %get-tuple-element.9.basis), custom_call_target="tpu_custom_call" | custom-call | tf_op jit(solution)/shard_map/update/pallas_call | solution.py:356

commit v5 on v4

--- a/solution.py
+++ b/solution.py
@@ -10,7 +10,7 @@
 SUB = 8
 PLANE = 4
 BLOCK = 128
-CHUNKS = 2
+CHUNKS = 4
 
 
 def matmul(left, right):
@@ -310,6 +310,8 @@
     basis = dot_exact(full(pblocks, row), linv, NT)
     basis_out[...] = basis
     rowside[:, :width] = dot_exact(basis, linv, NN)
+    solved = dot_exact(dot_exact(full(wblocks, row), linv, NT), linv, NN)
+    work[:, :width] = dot_exact(linv, linv, TN)
     for step, at in wsteps:
         step(*at)
     hswap = swap(proj, hrecv, 2)
@@ -318,8 +320,9 @@
     wstore.start()
     hswap.wait()
     total = proj[...] + hrecv[...]
-    rest = full(wblocks, row) - dot_exact(rowside[:, :width], total, NN)
-    rowside[:, width:] = dot_exact(dot_exact(rest, linv, NT), linv, NN)
+    rowside[:, width:] = solved - dot_exact(
+        rowside[:, :width], dot_exact(total, work[:, :width], NN), NN
+    )
     pgather.finish()
     wgather.finish()
     pstore.wait()

time: 121 us -> 137 us (1.13)
  Pallas kernels: 120 us -> 136 us
    pallas_call x1, Pallas kernels: 106 us -> 122 us  [fused(): pl.pallas_call(functools.partial(kernel, planes), out_shape=tuple((jax.Sh...]
where the time goes in v5:
time: 137 us
  Pallas kernels  136 us (99%)
    pallas_call x1, Pallas kernels, fused(): pl.pallas_call(functools.partial(kernel, planes), out_shape=tuple((jax.Sh...  122 us
    pallas_call x1, Pallas kernels, update(): pl.pallas_call(update_kernel, grid=(blocks,), out_shape=(jax.ShapeDtypeSt...  14.8 us

profile of v5, /device:TPU:0, one launch (start us, length us, event | category | flops | bytes accessed | tf_op | source)
XLA Modules:
  0.0 137.0 jit_solution(3574372929315098123)
XLA Ops:
  0.6 121.6 %panel_update.1 = (f32[2,8,512,128]{3,2,1,0:T(8,128)}, f32[2,8,512,128]{3,2,1,0:T(8,128)}, f32[512,512]{1,0:T(8,128)}, f32[512,256]{1,0:T(8,128)}) custom-call(f32[512,4096]{1,0:T(8,128)} %trailing.3, f32[512,128]{1,0:T(8,128)} %panel.1), custom_call_target="tpu_custom_call" | custom-call | tf_op jit(solution)/shard_map/panel_update/pallas_call | solution.py:381
  122.2 14.8 %update.1 = (f32[512,4096]{1,0:T(8,128)}, f32[512,256]{1,0:T(8,128)}) custom-call(f32[512,4096]{1,0:T(8,128)} %trailing.3, f32[2,8,512,128]{3,2,1,0:T(8,128)} %get-tuple-element.6.pcols, f32[2,8,512,128]{3,2,1,0:T(8,128)} %get-tuple-element.7.wcols, f32[512,512]{1,0:T(8,128)} %get-tuple-element.8.rowside, f32[512,256]{1,0:T(8,128)} %get-tuple-element.9.basis), custom_call_target="tpu_custom_call" | custom-call | tf_op jit(solution)/shard_map/update/pallas_call | solution.py:359

commit v6 on v5

--- a/solution.py
+++ b/solution.py
@@ -10,7 +10,7 @@
 SUB = 8
 PLANE = 4
 BLOCK = 128
-CHUNKS = 4
+CHUNKS = 1
 
 
 def matmul(left, right):

time: 137 us -> 132 us (0.964)
  Pallas kernels: 136 us -> 130 us
    pallas_call x1, Pallas kernels: 122 us -> 115 us  [fused(): pl.pallas_call(functools.partial(kernel, planes), out_shape=tuple((jax.Sh...]
where the time goes in v6:
time: 132 us; the launch traced here: 131 us
  Pallas kernels  130 us (98%)
    pallas_call x1, Pallas kernels, fused(): pl.pallas_call(functools.partial(kernel, planes), out_shape=tuple((jax.Sh...  115 us
    pallas_call x1, Pallas kernels, update(): pl.pallas_call(update_kernel, grid=(blocks,), out_shape=(jax.ShapeDtypeSt...  14.8 us

profile of v6, /device:TPU:0, one launch (start us, length us, event | category | flops | bytes accessed | tf_op | source)
XLA Modules:
  0.0 130.9 jit_solution(3598064381986640194)
XLA Ops:
  0.6 115.5 %panel_update.1 = (f32[2,8,512,128]{3,2,1,0:T(8,128)}, f32[2,8,512,128]{3,2,1,0:T(8,128)}, f32[512,512]{1,0:T(8,128)}, f32[512,256]{1,0:T(8,128)}) custom-call(f32[512,4096]{1,0:T(8,128)} %trailing.3, f32[512,128]{1,0:T(8,128)} %panel.1), custom_call_target="tpu_custom_call" | custom-call | tf_op jit(solution)/shard_map/panel_update/pallas_call | solution.py:381
  116.1 14.8 %update.1 = (f32[512,4096]{1,0:T(8,128)}, f32[512,256]{1,0:T(8,128)}) custom-call(f32[512,4096]{1,0:T(8,128)} %trailing.3, f32[2,8,512,128]{3,2,1,0:T(8,128)} %get-tuple-element.6.pcols, f32[2,8,512,128]{3,2,1,0:T(8,128)} %get-tuple-element.7.wcols, f32[512,512]{1,0:T(8,128)} %get-tuple-element.8.rowside, f32[512,256]{1,0:T(8,128)} %get-tuple-element.9.basis), custom_call_target="tpu_custom_call" | custom-call | tf_op jit(solution)/shard_map/update/pallas_call | solution.py:359
